TPU v7x, 32 devices: a whole 2x2x4 slice. The times are simulated.
32 devices in a mesh: seq: 8 (over z, x), tensor: 4 (over y, core).
Axes of the slice: x: 2, y: 2, z: 4, core: 2. Of those that a mesh axis runs over, the one named last changes fastest.
Arguments:
- history: bfloat16 [2, 2, 2048, 8192], P(None, None, 'seq', 'tensor'), may hold values from -6 to 6
- gates: bfloat16 [2, 2, 32, 8192], P(None, None, 'seq', 'tensor'), may hold values from -6 to 6
- rates: float32 [2, 16, 8192], P(None, None, 'tensor'), may hold values from 0.00014648438 to 0.1
- residues: float32 [2, 16, 8192], P(None, None, 'tensor'), may hold values from -2.1 to 2.1
- freqs: float32 [2, 16, 8192], P(None, None, 'tensor'), may hold values from 0 to 3.14159
- w_out: bfloat16 [2, 8192, 8192], P(None, 'tensor', 'seq'), may hold values from -0.0625 to 0.0625
- lengths: int32 [2], replicated, may hold values from 128 to 1536, as said below
- tile_index: int32 [1], replicated, may hold values from 0 to 15
Outputs:
- mixed: bfloat16 [2, 2, 32, 8192], P(None, None, 'tensor', 'seq')
Inputs may be any that keep to these rules, and one draw needn't show every extreme that they name: `lengths`: each length is a multiple of 128; at least one genome has the largest length.
All inputs are finite; a program needn't handle non-finite values.
Results may differ from a plain program's by a relative error of at most 0.0049.
Values may be sent and summed in bfloat16 or wider, within the bound.
A program may use at most 64 MiB of HBM per device.

v0:
```python
import jax
import jax.numpy as jnp
from jax import lax
from jax.sharding import PartitionSpec as P

LAYERS = 2


def lag_states(x_g, t0, positions, rate, freq):
    lag = t0 - positions
    live = lag > 0
    steps = jnp.where(live, lag, 0)
    steps_f = steps.astype(jnp.float32)
    values = jnp.where(live[:, None], x_g.astype(jnp.float32), jnp.float32(0.0))
    chans = values.shape[1]
    width = min(chans, 256)
    count = chans // width
    blocks_x = values.reshape(values.shape[0], count, width).transpose(1, 0, 2)
    blocks_r = rate.reshape(rate.shape[0], count, width).transpose(1, 0, 2)
    blocks_f = freq.reshape(freq.shape[0], count, width).transpose(1, 0, 2)

    def per_block(item):
        xb, rb, fb = item
        decay = jnp.exp(-rb[None, :, :] * steps_f[:, None, None])
        angle = fb[None, :, :] * steps_f[:, None, None]
        scaled = decay * xb[:, None, :]
        return (jnp.sum(scaled * jnp.cos(angle), axis=0), jnp.sum(scaled * jnp.sin(angle), axis=0))

    real_part, imag_part = lax.map(per_block, (blocks_x, blocks_r, blocks_f))
    real_part = real_part.transpose(1, 0, 2).reshape(rate.shape[0], chans)
    imag_part = imag_part.transpose(1, 0, 2).reshape(rate.shape[0], chans)
    return (real_part, imag_part)


def row_tables(rate, resid, freq, rows):
    rows_f = rows.astype(jnp.float32)
    amplitude = resid[None] * jnp.sqrt(rate)[None] * jnp.exp(-rate[None] * rows_f[:, None, None])
    angle = freq[None] * rows_f[:, None, None]
    return (amplitude * jnp.cos(angle), amplitude * jnp.sin(angle))


def shards(history, gates, rates, residues, freqs, w_out, lengths, tile_index):
    pos_dev = history.shape[2]
    rows_dev = gates.shape[2]
    seq_size = lax.axis_size("seq")
    seq_at = lax.axis_index("seq")
    tile = rows_dev * seq_size
    flush_at = lengths + tile * tile_index[0]
    first = seq_at * pos_dev
    positions = first + jnp.arange(pos_dev, dtype=jnp.int32)
    outputs = []
    for layer in range(LAYERS):
        rate = rates[layer]
        resid = residues[layer]
        freq = freqs[layer]
        weight = w_out[layer]

        def genome_states(item):
            x_g, t0 = item
            return lag_states(x_g, t0, positions, rate, freq)

        real_part, imag_part = lax.map(genome_states, (history[layer], flush_at))
        rows = jnp.arange(rows_dev * lax.axis_size("seq"), dtype=jnp.int32)
        table_re, table_im = row_tables(rate, resid, freq, rows)
        term = jnp.einsum("jmc,gmc->jgc", table_re, real_part, precision=lax.Precision.HIGHEST)
        summed = lax.psum_scatter(
            term - jnp.einsum("jmc,gmc->jgc", table_im, imag_part, precision=lax.Precision.HIGHEST),
            "seq",
            scatter_dimension=0,
            tiled=True,
        )
        contrib = summed.transpose(1, 0, 2)
        gated = (contrib * gates[layer].astype(jnp.float32)).astype(jnp.bfloat16)
        partial_out = jnp.einsum(
            "gjc,cd->gjd",
            lax.all_gather(gated, "seq", axis=1, tiled=True),
            weight,
            preferred_element_type=jnp.float32,
        )
        mixed = lax.psum_scatter(partial_out, "tensor", scatter_dimension=1, tiled=True)
        outputs.append(mixed.astype(jnp.bfloat16))
    return jnp.stack(outputs, axis=0)


def solution(mesh):
    in_specs = (
        P(None, None, "seq", "tensor"),
        P(None, None, "seq", "tensor"),
        P(None, None, "tensor"),
        P(None, None, "tensor"),
        P(None, None, "tensor"),
        P(None, "tensor", "seq"),
        P(),
        P(),
    )
    out_specs = P(None, None, "tensor", "seq")
    return jax.shard_map(shards, mesh=mesh, in_specs=in_specs, out_specs=out_specs, check_vma=False)
```

profile of v0, /device:TPU:0, one launch (start us, length us, event | category | flops | bytes accessed | tf_op | source)
XLA Modules:
  0.0 1128.9 jit_solution(3416741492658118959)
XLA Ops:
  16.2 285.7 %while.53 = (s32[]{:T(128)}, f32[2,16,2048]{2,1,0:T(8,128)}, f32[2,16,2048]{2,1,0:T(8,128)}, s32[2]{0:T(128)S(1)}, bf16[2,256,2048]{1,2,0:T(8,128)(2,1)}, /*inde...) while((s32[]{:T(128)}, f32[2,16,2048]{2,1,0:T(8,128)}, ...), condition=%wide.region_5.6_spmd.clone, body=%wide.region_0.5_spmd.clone.sunk | while | flops 8386564 | bytes 8916790 | solution.py:62
  19.8 137.5 %while.56 = (s32[]{:T(128)}, f32[8,16,256]{2,1,0:T(8,128)S(1)}, f32[8,16,256]{2,1,0:T(8,128)}, f32[8,16,256]{2,0,1:T(8,128)S(1)}, f32[256]{0:T(256)S(1)}, /*inde...) while((s32[]{:T(128)}, f32[8,16,256]{2,1,0:T(8,128)S(1)}, f32[8,16,256]{2,1,0:T(8,128)}, ...), condition=%wide.region_4.4_spmd, body=%wide.region_1.3_spmd.sunk | while | flops 7335938 | bytes 1574497 | solution.py:29
  54.4 16.3 %fusion.100 = (f32[16,256]{1,0:T(8,128)S(1)}, f32[16,256]{1,0:T(8,128)S(1)}) fusion(f32[16,256]{1,0:T(8,128)S(1)} %bitcast.166, f32[256,256]{1,0:T(8,128)S(1)} %bitcast.162, f32[256]{0:T(256)S(1)} %get-tuple-element.637, f32[16,256]{1,0:T(8,128)S(1)} %fusion.99), kind=kLoop, calls=%fused_computation.7.clone.1 | loop fusion | flops 7331840 | bytes 328704 | tf_op jit(solution)/shard_map/while/body/eval_jaxpr/while/body/eval_jaxpr/reduce_sum | solution.py:27
  105.9 16.3 %fusion.100 = (f32[16,256]{1,0:T(8,128)S(1)}, f32[16,256]{1,0:T(8,128)S(1)}) fusion(f32[16,256]{1,0:T(8,128)S(1)} %bitcast.166, f32[256,256]{1,0:T(8,128)S(1)} %bitcast.162, f32[256]{0:T(256)S(1)} %get-tuple-element.637, f32[16,256]{1,0:T(8,128)S(1)} %fusion.99), kind=kLoop, calls=%fused_computation.7.clone.1 | loop fusion | flops 7331840 | bytes 328704 | tf_op jit(solution)/shard_map/while/body/eval_jaxpr/while/body/eval_jaxpr/reduce_sum | solution.py:27
  123.1 16.3 %fusion.100 = (f32[16,256]{1,0:T(8,128)S(1)}, f32[16,256]{1,0:T(8,128)S(1)}) fusion(f32[16,256]{1,0:T(8,128)S(1)} %bitcast.166, f32[256,256]{1,0:T(8,128)S(1)} %bitcast.162, f32[256]{0:T(256)S(1)} %get-tuple-element.637, f32[16,256]{1,0:T(8,128)S(1)} %fusion.99), kind=kLoop, calls=%fused_computation.7.clone.1 | loop fusion | flops 7331840 | bytes 328704 | tf_op jit(solution)/shard_map/while/body/eval_jaxpr/while/body/eval_jaxpr/reduce_sum | solution.py:27
  140.3 16.3 %fusion.100 = (f32[16,256]{1,0:T(8,128)S(1)}, f32[16,256]{1,0:T(8,128)S(1)}) fusion(f32[16,256]{1,0:T(8,128)S(1)} %bitcast.166, f32[256,256]{1,0:T(8,128)S(1)} %bitcast.162, f32[256]{0:T(256)S(1)} %get-tuple-element.637, f32[16,256]{1,0:T(8,128)S(1)} %fusion.99), kind=kLoop, calls=%fused_computation.7.clone.1 | loop fusion | flops 7331840 | bytes 328704 | tf_op jit(solution)/shard_map/while/body/eval_jaxpr/while/body/eval_jaxpr/reduce_sum | solution.py:27
  162.6 137.5 %while.56 = (s32[]{:T(128)}, f32[8,16,256]{2,1,0:T(8,128)S(1)}, f32[8,16,256]{2,1,0:T(8,128)}, f32[8,16,256]{2,0,1:T(8,128)S(1)}, f32[256]{0:T(256)S(1)}, /*inde...) while((s32[]{:T(128)}, f32[8,16,256]{2,1,0:T(8,128)S(1)}, f32[8,16,256]{2,1,0:T(8,128)}, ...), condition=%wide.region_4.4_spmd, body=%wide.region_1.3_spmd.sunk | while | flops 7335938 | bytes 1574497 | solution.py:29
  197.2 16.3 %fusion.100 = (f32[16,256]{1,0:T(8,128)S(1)}, f32[16,256]{1,0:T(8,128)S(1)}) fusion(f32[16,256]{1,0:T(8,128)S(1)} %bitcast.166, f32[256,256]{1,0:T(8,128)S(1)} %bitcast.162, f32[256]{0:T(256)S(1)} %get-tuple-element.637, f32[16,256]{1,0:T(8,128)S(1)} %fusion.99), kind=kLoop, calls=%fused_computation.7.clone.1 | loop fusion | flops 7331840 | bytes 328704 | tf_op jit(solution)/shard_map/while/body/eval_jaxpr/while/body/eval_jaxpr/reduce_sum | solution.py:27
  248.8 16.3 %fusion.100 = (f32[16,256]{1,0:T(8,128)S(1)}, f32[16,256]{1,0:T(8,128)S(1)}) fusion(f32[16,256]{1,0:T(8,128)S(1)} %bitcast.166, f32[256,256]{1,0:T(8,128)S(1)} %bitcast.162, f32[256]{0:T(256)S(1)} %get-tuple-element.637, f32[16,256]{1,0:T(8,128)S(1)} %fusion.99), kind=kLoop, calls=%fused_computation.7.clone.1 | loop fusion | flops 7331840 | bytes 328704 | tf_op jit(solution)/shard_map/while/body/eval_jaxpr/while/body/eval_jaxpr/reduce_sum | solution.py:27
  265.9 16.3 %fusion.100 = (f32[16,256]{1,0:T(8,128)S(1)}, f32[16,256]{1,0:T(8,128)S(1)}) fusion(f32[16,256]{1,0:T(8,128)S(1)} %bitcast.166, f32[256,256]{1,0:T(8,128)S(1)} %bitcast.162, f32[256]{0:T(256)S(1)} %get-tuple-element.637, f32[16,256]{1,0:T(8,128)S(1)} %fusion.99), kind=kLoop, calls=%fused_computation.7.clone.1 | loop fusion | flops 7331840 | bytes 328704 | tf_op jit(solution)/shard_map/while/body/eval_jaxpr/while/body/eval_jaxpr/reduce_sum | solution.py:27
  283.1 16.3 %fusion.100 = (f32[16,256]{1,0:T(8,128)S(1)}, f32[16,256]{1,0:T(8,128)S(1)}) fusion(f32[16,256]{1,0:T(8,128)S(1)} %bitcast.166, f32[256,256]{1,0:T(8,128)S(1)} %bitcast.162, f32[256]{0:T(256)S(1)} %get-tuple-element.637, f32[16,256]{1,0:T(8,128)S(1)} %fusion.99), kind=kLoop, calls=%fused_computation.7.clone.1 | loop fusion | flops 7331840 | bytes 328704 | tf_op jit(solution)/shard_map/while/body/eval_jaxpr/while/body/eval_jaxpr/reduce_sum | solution.py:27
  312.4 86.9 %fusion.23 = f32[2048,2,32]{2,1,0:T(2,128)S(1)} fusion(f32[2,16,2048]{1,0,2:T(2,128)S(1)} %copy.67, f32[16,2048]{0,1:T(8,128)} %copy.66, f32[32]{0:T(128)S(1)} %iota_convert_fusion, f32[16,2048]{0,1:T(8,128)} %copy.65, f32[16,2048]{0,1:T(8,128)} %copy.64), kind=kOutput, calls=%fused_computation.55 | convolution fusion | flops 29360128 | bytes 1179776 | tf_op jit(solution)/shard_map/jmc,gmc->jgc/dot_general | solution.py:65
  399.4 85.4 %subtract_bitcast_fusion.1 = f32[32,2,2048]{0,1,2:T(2,128)} fusion(f32[2048,2,32]{2,1,0:T(2,128)S(1)} %fusion.23, f32[2,16,2048]{1,0,2:T(2,128)S(1)} %copy-done.2, f32[16,2048]{0,1:T(8,128)S(1)} %copy-done.9, f32[32]{0:T(128)S(1)} %iota_convert_fusion, f32[16,2048]{0,1:T(8,128)S(1)} %copy-done.7, f32[16,2048]{0,1:T(8,128)S(1)} %copy-done.6), kind=kOutput, calls=%fused_computation.87 | convolution fusion | flops 29491200 | bytes 1704064 | tf_op jit(solution)/shard_map/jmc,gmc->jgc/dot_general | solution.py:67
  492.6 274.9 %while.55 = (s32[]{:T(128)}, f32[2,16,2048]{2,1,0:T(8,128)}, f32[2,16,2048]{2,1,0:T(8,128)}, s32[2]{0:T(128)S(1)}, bf16[2,256,2048]{1,2,0:T(8,128)(2,1)}, /*inde...) while((s32[]{:T(128)}, f32[2,16,2048]{2,1,0:T(8,128)}, ...), condition=%wide.region_13.14_spmd.clone, body=%wide.region_8.13_spmd.clone.sunk | while | flops 8386564 | bytes 8916282 | solution.py:62
  496.1 132.9 %while.57 = (s32[]{:T(128)}, f32[8,16,256]{2,1,0:T(8,128)S(1)}, f32[8,16,256]{2,1,0:T(8,128)S(1)}, f32[8,16,256]{2,0,1:T(8,128)S(1)}, f32[256]{0:T(256)S(1)}, /*...) while((s32[]{:T(128)}, f32[8,16,256]{2,1,0:T(8,128)S(1)}, ...), condition=%wide.region_12.12_spmd, body=%wide.region_9.11_spmd.sunk | while | flops 7335938 | bytes 1573989 | solution.py:29
  496.4 16.3 %fusion.98 = (f32[16,256]{1,0:T(8,128)S(1)}, f32[16,256]{1,0:T(8,128)S(1)}) fusion(f32[16,256]{1,0:T(8,128)S(1)} %bitcast.167, f32[256,256]{1,0:T(8,128)S(1)} %bitcast.163, f32[256]{0:T(256)S(1)} %get-tuple-element.613, f32[16,256]{1,0:T(8,128)S(1)} %fusion.97), kind=kLoop, calls=%fused_computation.22.clone.1 | loop fusion | flops 7331840 | bytes 328704 | tf_op jit(solution)/shard_map/while/body/eval_jaxpr/while/body/eval_jaxpr/reduce_sum | solution.py:27
  546.2 16.3 %fusion.98 = (f32[16,256]{1,0:T(8,128)S(1)}, f32[16,256]{1,0:T(8,128)S(1)}) fusion(f32[16,256]{1,0:T(8,128)S(1)} %bitcast.167, f32[256,256]{1,0:T(8,128)S(1)} %bitcast.163, f32[256]{0:T(256)S(1)} %get-tuple-element.613, f32[16,256]{1,0:T(8,128)S(1)} %fusion.97), kind=kLoop, calls=%fused_computation.22.clone.1 | loop fusion | flops 7331840 | bytes 328704 | tf_op jit(solution)/shard_map/while/body/eval_jaxpr/while/body/eval_jaxpr/reduce_sum | solution.py:27
  633.6 132.9 %while.57 = (s32[]{:T(128)}, f32[8,16,256]{2,1,0:T(8,128)S(1)}, f32[8,16,256]{2,1,0:T(8,128)S(1)}, f32[8,16,256]{2,0,1:T(8,128)S(1)}, f32[256]{0:T(256)S(1)}, /*...) while((s32[]{:T(128)}, f32[8,16,256]{2,1,0:T(8,128)S(1)}, ...), condition=%wide.region_12.12_spmd, body=%wide.region_9.11_spmd.sunk | while | flops 7335938 | bytes 1573989 | solution.py:29
  777.0 86.4 %fusion.29 = f32[2048,2,32]{2,1,0:T(2,128)S(1)} fusion(f32[2,16,2048]{1,0,2:T(2,128)S(1)} %copy.76, f32[16,2048]{0,1:T(8,128)} %copy.75, f32[16,2048]{0,1:T(8,128)} %copy.74, f32[16,2048]{0,1:T(8,128)S(1)} %copy.73, f32[32]{0:T(128)S(1)} %iota_convert_fusion), kind=kOutput, calls=%fused_computation.59 | convolution fusion | flops 29360128 | bytes 1179776 | tf_op jit(solution)/shard_map/jmc,gmc->jgc/dot_general | solution.py:65
  863.5 84.5 %subtract_bitcast_fusion = f32[32,2,2048]{0,1,2:T(2,128)S(1)} fusion(f32[2048,2,32]{2,1,0:T(2,128)S(1)} %fusion.29, f32[2,16,2048]{1,0,2:T(2,128)S(1)} %copy-done.1, f32[16,2048]{0,1:T(8,128)S(1)} %copy-done.8, f32[16,2048]{0,1:T(8,128)S(1)} %copy-done.5, f32[16,2048]{0,1:T(8,128)S(1)} %copy.73, f32[32]{0:T(128)S(1)} %iota_convert_fusion), kind=kOutput, calls=%fused_computation.86 | convolution fusion | flops 29491200 | bytes 1704064 | tf_op jit(solution)/shard_map/jmc,gmc->jgc/dot_general | solution.py:67
  951.3 79.8 %all-reduce.5.cloned.1.call-done = (f32[32,2,2048]{2,0,1:T(8,128)}, f32[32,2,2048]{2,0,1:T(8,128)}) async-done(((f32[32,2,2048]{2,0,1:T(8,128)}, f32[32,2,2048]{2,0,1:T(8,128)}), (f32[32,2,2048]{2,0,1:T(8,128)}, f32[32,2,2048]{2,0,1:T(8,128)})) %all-reduce.5.cloned.1.call-update) | async-done | bytes 1048592
  1032.2 30.8 %all_gather.7 = bf16[2,32,2048]{2,0,1:T(2,128)(2,1)S(1)} all-gather(bf16[2,4,2048]{2,0,1:T(2,128)(2,1)S(1)} %copy.79), channel_id=1, replica_groups=mesh['seq'=8,'tensor'=4] {'seq'}, dimensions={1}, use_global_device_ids=true | all-gather | bytes 294912 | tf_op jit(solution)/shard_map/all_gather | solution.py:76
  1066.8 30.7 %all_gather.6 = bf16[2,32,2048]{2,0,1:T(2,128)(2,1)S(1)} all-gather(bf16[2,4,2048]{2,0,1:T(2,128)(2,1)S(1)} %copy.70), channel_id=1, replica_groups=mesh['seq'=8,'tensor'=4] {'seq'}, dimensions={1}, use_global_device_ids=true | all-gather | bytes 294912 | tf_op jit(solution)/shard_map/all_gather | solution.py:76
  1102.2 18.6 %reduce-scatter.5.cloned.1.call-done = f32[2,8,1024]{2,1,0:T(8,128)} async-done(((f32[2,32,1024]{2,1,0:T(8,128)}), f32[2,8,1024]{2,1,0:T(8,128)}) %reduce-scatter.5.cloned.1.call-update) | async-done | bytes 65552 | tf_op jit(solution)/shard_map/reduce_scatter | solution.py:80
  (376 shorter events, 445.3 us)
Async XLA Ops:
  6.5 1024.6 %all-reduce.5.cloned.1.call-start = ((), (), s32[]{:S(2)}) async-start(), calls=%async_computation.4 | async-start | bytes 2097152
  10.5 3.2 copy-start.16
  10.6 3.2 copy-start.12
  10.6 3.2 copy-start.13
  10.6 3.2 copy-start.14
  301.9 6.9 copy-start.11
  301.9 8.3 copy-start.4
  312.4 86.9 %copy-start.2 = (f32[2,16,2048]{1,0,2:T(2,128)S(1)}, f32[2,16,2048]{1,0,2:T(2,128)}, u32[]{:S(2)}) copy-start(f32[2,16,2048]{1,0,2:T(2,128)} %copy.68) | copy-start | bytes 786436
  312.4 86.9 %copy-start.6 = (f32[16,2048]{0,1:T(8,128)S(1)}, f32[16,2048]{0,1:T(8,128)}, u32[]{:S(2)}) copy-start(f32[16,2048]{0,1:T(8,128)} %copy.64) | copy-start | bytes 393220
  312.4 86.9 %copy-start.7 = (f32[16,2048]{0,1:T(8,128)S(1)}, f32[16,2048]{0,1:T(8,128)}, u32[]{:S(2)}) copy-start(f32[16,2048]{0,1:T(8,128)} %copy.65) | copy-start | bytes 393220
  312.4 86.9 %copy-start.9 = (f32[16,2048]{0,1:T(8,128)S(1)}, f32[16,2048]{0,1:T(8,128)}, u32[]{:S(2)}) copy-start(f32[16,2048]{0,1:T(8,128)} %copy.66) | copy-start | bytes 393220
  399.3 89.3 %copy-start = (bf16[1,2,256,2048]{3,2,1,0:T(8,128)(2,1)S(1)}, bf16[1,2,256,2048]{3,2,1,0:T(8,128)(2,1)}, u32[]{:S(2)}) copy-start(bf16[1,2,256,2048]{3,2,1,0:T(8,128)(2,1)} %get-tuple-element.330) | copy-start | bytes 6291460
  767.5 6.0 copy-start.10
  767.5 7.3 copy-start.3
  777.0 86.4 %copy-start.1 = (f32[2,16,2048]{1,0,2:T(2,128)S(1)}, f32[2,16,2048]{1,0,2:T(2,128)}, u32[]{:S(2)}) copy-start(f32[2,16,2048]{1,0,2:T(2,128)} %copy.77) | copy-start | bytes 786436
  777.0 86.4 %copy-start.5 = (f32[16,2048]{0,1:T(8,128)S(1)}, f32[16,2048]{0,1:T(8,128)}, u32[]{:S(2)}) copy-start(f32[16,2048]{0,1:T(8,128)} %copy.74) | copy-start | bytes 393220
  777.0 86.4 %copy-start.8 = (f32[16,2048]{0,1:T(8,128)S(1)}, f32[16,2048]{0,1:T(8,128)}, u32[]{:S(2)}) copy-start(f32[16,2048]{0,1:T(8,128)} %copy.75) | copy-start | bytes 393220
  863.4 86.6 %copy-start.17 = (u32[32]{0:T(128)S(1)}, u32[32]{0:T(128)}, u32[]{:S(2)}) copy-start(u32[32]{0:T(128)} %constant.73) | copy-start | bytes 388
  863.5 167.7 %copy-start.15 = (bf16[2,2,4,2048]{3,2,1,0:T(4,128)(2,1)S(1)}, bf16[2,2,4,2048]{3,2,1,0:T(4,128)(2,1)}, u32[]{:S(2)}) copy-start(bf16[2,2,4,2048]{3,2,1,0:T(4,128)(2,1)} %param.17) | copy-start | bytes 196612
  950.0 151.4 %reduce-scatter.7.cloned.1.call-start = ((), (), s32[]{:S(2)}) async-start(), calls=%async_computation.3 | async-start | bytes 327680 | tf_op jit(solution)/shard_map/reduce_scatter | solution.py:80
  1066.7 54.1 %reduce-scatter.5.cloned.1.call-start = ((), (), s32[]{:S(2)}) async-start(), calls=%async_computation.2 | async-start | bytes 327680 | tf_op jit(solution)/shard_map/reduce_scatter | solution.py:80
Sparse Core Ops, SparseCore 0:
  950.1 80.9 all-reduce.4
  1066.9 19.3 reduce-scatter.6
  1101.4 19.3 reduce-scatter.4
where the time goes:
time: 1130 us
  other arithmetic  533 us (47%)
  matrix products  351 us (31%)
  waiting for transfers between devices  98.6 us (9%)
  local copies, waits for them, and re-layouts  68.1 us (6%)
  blocking collectives  61.6 us (5%)
  between operations  14.6 us (1%)
    reduce_sum x32, other arithmetic, per_block(): jnp.sum(scaled * jnp.sin(angle), axis=0)  523 us
    dot_general x2, matrix products, shards(): jnp.einsum('jmc,gmc->jgc', table_re, real_part, precision=lax.Precision.H...  173 us
    dot_general x2, matrix products, shards(): jnp.einsum('jmc,gmc->jgc', table_im, imag_part, precision=lax.Precision.H...  170 us
    unnamed x4, waiting for transfers between devices  79.9 us
    all_gather x2, blocking collectives, shards(): lax.all_gather(gated, 'seq', axis=1, tiled=True)  61.6 us
  transfers between devices with their start and end apart: 3, of which 2 were waited for; matrix products, arithmetic and copies ran while one was open for 0% of the time, Pallas kernels for 0%

commit v1 on v0

v1 whole, which is shorter than its diff:
```python
import functools
import math

import jax
import jax.numpy as jnp
from jax import lax
from jax.experimental import pallas as pl
from jax.experimental.pallas import tpu as pltpu
from jax.sharding import PartitionSpec as P

UNIT = 128
SUB = 8
LANE = 128
GROUP = 4
STEPS = 64
RUN = 32


def cmul(ar, ai, br, bi):
    return ar * br - ai * bi, ar * bi + ai * br


def csq(ar, ai):
    return ar * ar - ai * ai, 2.0 * (ar * ai)


def cos_sin(angle):
    y = (angle - 1.57079637050628662) + 4.37113883e-8
    y2 = y * y
    s = jnp.full_like(y, 1.0 / math.factorial(13))
    for n, sign in ((11, -1), (9, 1), (7, -1), (5, 1), (3, -1), (1, 1)):
        s = s * y2 + sign / math.factorial(n)
    c = jnp.full_like(y, -1.0 / math.factorial(14))
    for n, sign in ((12, 1), (10, -1), (8, 1), (6, -1), (4, 1), (2, -1), (0, 1)):
        c = c * y2 + sign / math.factorial(n)
    return -(s * y), c


def spread_rows(dst, base, value):
    count = value.shape[0]
    for k in range(SUB):
        dst[pl.ds(base + k, count, stride=SUB), :] = value[:, k * LANE:(k + 1) * LANE]


def local_kernel(granule, bits, info, x_ref, rate_ref, resid_ref, freq_ref, out_ref, xs, pars):
    genomes, span = x_ref.shape[1], x_ref.shape[2]
    modes = rate_ref.shape[1]
    rows = out_ref.shape[1]
    chunk = 32
    first = info[genomes]
    for i, ref in enumerate((rate_ref, resid_ref, freq_ref)):
        spread_rows(pars.at[i], 0, ref[0])
    hops = []
    for g in range(genomes):
        live = jnp.minimum(jnp.maximum(info[g] - first, 0), span)
        hops.append(lax.div(jnp.maximum(info[g] - first - live, 0), granule))

        @pl.loop(0, span // chunk)
        def _(q):
            src = q * chunk - (span - live)
            block = x_ref[0, g, pl.ds(pl.multiple_of(jnp.maximum(src, 0), chunk), chunk), :]
            block = jnp.where(src >= 0, block.astype(jnp.float32), 0.0)
            spread_rows(xs.at[g], q * (chunk * SUB), block)

    out_ref[...] = jnp.zeros_like(out_ref)
    wide = GROUP * SUB

    @pl.loop(0, modes // GROUP)
    def _(mg):
        at = pl.ds(pl.multiple_of(mg * wide, wide), wide)
        rate, resid, freq = pars[0, at, :], pars[1, at, :], pars[2, at, :]
        decay = jnp.exp(-rate)
        c, s = cos_sin(freq)
        zr, zi = decay * c, decay * s
        trace, norm = 2.0 * zr, zr * zr + zi * zi
        amp = resid * jnp.sqrt(rate)

        def cut(v):
            return [v[i * SUB:(i + 1) * SUB] for i in range(GROUP)]

        zr_c, zi_c, tr_c, no_c = cut(zr), cut(zi), cut(trace), cut(norm)
        pr, pi = zr, zi
        for _ in range(int(math.log2(STEPS))):
            pr, pi = csq(pr, pi)
        br_c, bi_c = cut(pr), cut(pi)
        n_state = genomes * GROUP
        zero = jnp.zeros((SUB, LANE), jnp.float32)

        def block_step(blk, carry):
            re, im = carry
            a = [zero] * n_state
            b = [zero] * n_state
            for t in range(STEPS):
                for g in range(genomes):
                    x = xs[g, pl.ds(pl.multiple_of(blk * (STEPS * SUB) + t * SUB, SUB), SUB), :]
                    for i in range(GROUP):
                        k = g * GROUP + i
                        a[k], b[k] = b[k] + tr_c[i] * a[k], x - no_c[i] * a[k]
            new_re, new_im = [], []
            for g in range(genomes):
                for i in range(GROUP):
                    k = g * GROUP + i
                    sr, si = cmul(br_c[i], bi_c[i], re[k], im[k])
                    new_re.append(sr + (zr_c[i] * a[k] + b[k]))
                    new_im.append(si + zi_c[i] * a[k])
            return tuple(new_re), tuple(new_im)

        init = ((zero,) * n_state, (zero,) * n_state)
        re, im = lax.fori_loop(0, span // STEPS, block_step, init)

        pr, pi = zr, zi
        for _ in range(int(math.log2(granule))):
            pr, pi = csq(pr, pi)
        lead_r, lead_i = amp * zr, amp * zi
        far = [(lead_r, lead_i) for _ in range(genomes)]
        for bit in range(bits):
            for g in range(genomes):
                fr, fi = far[g]
                nr, ni = cmul(fr, fi, pr, pi)
                on = lax.rem(lax.div(hops[g], 1 << bit), 2) == 1
                far[g] = (jnp.where(on, nr, fr), jnp.where(on, ni, fi))
            if bit + 1 < bits:
                pr, pi = csq(pr, pi)
        start = []
        for g in range(genomes):
            fr, fi = cut(far[g][0]), cut(far[g][1])
            start.append([cmul(re[g * GROUP + i], im[g * GROUP + i], fr[i], fi[i]) for i in range(GROUP)])
        qr, qi = zr, zi
        for _ in range(int(math.log2(RUN))):
            qr, qi = csq(qr, qi)
        qr_c, qi_c = cut(qr), cut(qi)

        def row_run(run, carry):
            wr, wi = carry
            base = run * RUN
            old = [None] * n_state
            now = list(wr)
            for j in range(RUN):
                for g in range(genomes):
                    total = now[g * GROUP]
                    for i in range(1, GROUP):
                        total = total + now[g * GROUP + i]
                    out_ref[0, base + j, g] += total
                for g in range(genomes):
                    for i in range(GROUP):
                        k = g * GROUP + i
                        if j == 0:
                            nxt = wr[k] * zr_c[i] - wi[k] * zi_c[i]
                        else:
                            nxt = tr_c[i] * now[k] - no_c[i] * old[k]
                        old[k], now[k] = now[k], nxt
            moved = [cmul(wr[g * GROUP + i], wi[g * GROUP + i], qr_c[i], qi_c[i])
                     for g in range(genomes) for i in range(GROUP)]
            return tuple(m[0] for m in moved), tuple(m[1] for m in moved)

        wr = tuple(start[g][i][0] for g in range(genomes) for i in range(GROUP))
        wi = tuple(start[g][i][1] for g in range(genomes) for i in range(GROUP))
        lax.fori_loop(0, rows // RUN, row_run, (wr, wi))


def local_terms(info, history, rates, residues, freqs, rows, bits, granule):
    layers, genomes, span, chans = history.shape
    modes = rates.shape[1]
    wide = SUB * LANE
    par_spec = pl.BlockSpec((1, modes, wide), lambda l, c: (l, 0, c))
    return pl.pallas_call(
        functools.partial(local_kernel, granule, bits),
        grid=(layers, chans // wide),
        out_shape=jax.ShapeDtypeStruct((layers, rows, genomes, chans // LANE, LANE), jnp.float32),
        in_specs=[
            pl.BlockSpec(memory_space=pltpu.SMEM),
            pl.BlockSpec((1, genomes, span, wide), lambda l, c: (l, 0, 0, c)),
            par_spec, par_spec, par_spec,
        ],
        out_specs=pl.BlockSpec((1, rows, genomes, SUB, LANE), lambda l, c: (l, 0, 0, c, 0)),
        scratch_shapes=[
            pltpu.VMEM((genomes, span * SUB, LANE), jnp.float32),
            pltpu.VMEM((3, modes * SUB, LANE), jnp.float32),
        ],
        compiler_params=pltpu.CompilerParams(vmem_limit_bytes=48 * 1024 * 1024),
    )(info, history, rates, residues, freqs)


def shards(history, gates, rates, residues, freqs, w_out, lengths, tile_index):
    layers, genomes, span, chans = history.shape
    rows_dev = gates.shape[2]
    seq_size = lax.axis_size("seq")
    tile = rows_dev * seq_size
    granule = math.gcd(UNIT, tile)
    bits = (span * seq_size // granule).bit_length()
    flush_at = lengths + tile * tile_index[0]
    first = lax.axis_index("seq") * span
    info = jnp.concatenate([flush_at, first[None]]).astype(jnp.int32)
    term = local_terms(info, history, rates, residues, freqs, tile, bits, granule)
    summed = lax.psum_scatter(term, "seq", scatter_dimension=1, tiled=True)
    gates_t = gates.transpose(0, 2, 1, 3).astype(jnp.float32)
    gated = (summed.reshape(layers, rows_dev, genomes, chans) * gates_t).astype(jnp.bfloat16)
    full = lax.all_gather(gated, "seq", axis=1, tiled=True)
    partial_out = jnp.einsum("ljgc,lcd->lgjd", full, w_out, preferred_element_type=jnp.float32)
    mixed = lax.psum_scatter(partial_out, "tensor", scatter_dimension=2, tiled=True)
    return mixed.astype(jnp.bfloat16)


def solution(mesh):
    in_specs = (
        P(None, None, "seq", "tensor"),
        P(None, None, "seq", "tensor"),
        P(None, None, "tensor"),
        P(None, None, "tensor"),
        P(None, None, "tensor"),
        P(None, "tensor", "seq"),
        P(),
        P(),
    )
    out_specs = P(None, None, "tensor", "seq")
    return jax.shard_map(shards, mesh=mesh, in_specs=in_specs, out_specs=out_specs, check_vma=False)
```

time: 1130 us -> 193 us (0.17)
  other arithmetic: 533 us -> 3.23 us
  matrix products: 351 us -> 5.9 us
  local copies, waits for them, and re-layouts: 68.1 us -> 7.33 us
  blocking collectives: 61.6 us -> 31.4 us
  Pallas kernels: 0 us -> 30 us
    reduce_sum x32 -> x0, other arithmetic: 523 us -> none  [per_block(): jnp.sum(scaled * jnp.sin(angle), axis=0)]
    dot_general x6 -> x1, matrix products: 351 us -> 5.9 us  [shards(): jnp.einsum('ljgc,lcd->lgjd', full, w_out, preferred_element_type=jnp.floa...]
    all_gather x2 -> x1, blocking collectives: 61.6 us -> 31.4 us  [shards(): full = lax.all_gather(gated, 'seq', axis=1, tiled=True)]
    pallas_call x0 -> x1, Pallas kernels: none -> 30 us  [local_terms(): pl.pallas_call(functools.partial(local_kernel, granule, bits), grid=(laye...]
    dynamic_slice x168 -> x0, local copies, waits for them, and re-layouts: 13.8 us -> none  [the longest x8 7.77 us: shards(): real_part, imag_part = lax.map(genome_states, (history[layer], flush_at))]
    dynamic_update_slice x36 -> x0, local copies, waits for them, and re-layouts: 12.8 us -> none  [the longest x32 9.86 us: lag_states(): real_part, imag_part = lax.map(per_block, (blocks_x, blocks_r, blocks_f))]
    unnamed x4 -> x3, waiting for transfers between devices: 79.9 us -> 78.9 us
  transfers between devices with their start and end apart: 3 -> 2, of which waited for: 2 -> 2; matrix products, arithmetic and copies ran while one was open for 0% -> 1% of each run, Pallas kernels for 0% -> 0%
where the time goes in v1:
time: 193 us
  waiting for transfers between devices  100 us (52%)
  blocking collectives  31.4 us (16%)
  Pallas kernels  30 us (16%)
  between operations  14.7 us (8%)
  local copies, waits for them, and re-layouts  7.33 us (4%)
  matrix products  5.9 us (3%)
  other arithmetic  3.23 us (2%)
    unnamed x3, waiting for transfers between devices  78.9 us
    all_gather x1, blocking collectives, shards(): full = lax.all_gather(gated, 'seq', axis=1, tiled=True)  31.4 us
    pallas_call x1, Pallas kernels, local_terms(): pl.pallas_call(functools.partial(local_kernel, granule, bits), grid=(laye...  30 us
    reduce_scatter x1, waiting for transfers between devices, shards(): lax.psum_scatter(partial_out, 'tensor', scatter_dimension=2, tiled=True)  21.4 us
    unnamed x10, local copies, waits for them, and re-layouts  7.19 us
    dot_general x1, matrix products, shards(): jnp.einsum('ljgc,lcd->lgjd', full, w_out, preferred_element_type=jnp.floa...  5.9 us
  transfers between devices with their start and end apart: 2, of which 2 were waited for; matrix products, arithmetic and copies ran while one was open for 1% of the time, Pallas kernels for 0%

profile of v1, /device:TPU:0, one launch (start us, length us, event | category | flops | bytes accessed | tf_op | source)
XLA Modules:
  0.0 193.0 jit_solution(16312445141490654160)
XLA Ops:
  6.5 0.0 all-reduce.3.cloned.1.call-start
  7.2 0.7 broadcast_add_fusion
  7.8 0.1 pad_add_fusion.info
  7.9 0.0 copy-start
  7.9 2.2 %copy-done = bf16[2,2,256,2048]{3,2,1,0:T(8,128)(2,1)S(1)} copy-done((bf16[2,2,256,2048]{3,2,1,0:T(8,128)(2,1)S(1)}, bf16[2,2,256,2048]{3,2,1,0:T(8,128)(2,1)}, u32[]{:S(2)}) %copy-start) | copy-done | bytes 4194328
  10.1 0.0 copy-start.1
  10.1 0.9 copy-done.1
  11.1 0.0 copy-start.2
  11.1 0.9 copy-done.2
  12.0 0.9 copy-done.3
  13.0 30.0 %shard_map.82 = f32[2,32,2,16,128]{4,3,2,1,0:T(8,128)} custom-call(s32[3]{0:T(128)S(1)} %pad_add_fusion.info, bf16[2,2,256,2048]{3,2,1,0:T(8,128)(2,1)S(1)} %copy-done, f32[2,16,2048]{2,1,0:T(8,128)S(1)} %copy-done.1, f32[2,16,2048]{2,1,0:T(8,128)S(1)} %copy-done.2, f32[2,16,2048]{2,1,0:T(8,128)S(1)} %copy-done.3), custom_call_target="tpu_custom_call" | custom-call | tf_op jit(solution)/shard_map/pallas_call | solution.py:166
  43.0 0.0 all-reduce.3.cloned.1.call-update
  43.0 0.0 reduce-scatter.5.cloned.1.call-start
  43.1 1.2 dynamic-slice
  45.0 78.9 %all-reduce.3.cloned.1.call-done = f32[2,32,2,16,128]{4,3,2,1,0:T(8,128)} async-done(((f32[2,32,2,16,128]{4,3,2,1,0:T(8,128)}), f32[2,32,2,16,128]{4,3,2,1,0:T(8,128)}) %all-reduce.3.cloned.1.call-update) | async-done | bytes 1048592
  123.9 0.9 constant_dynamic-slice_fusion
  124.8 0.1 reshape.7
  124.8 0.9 fusion.6
  125.8 0.1 copy.14
  125.9 31.4 %all_gather.3 = bf16[2,32,2,2048]{3,2,0,1:T(2,128)(2,1)S(1)} all-gather(bf16[2,4,2,2048]{3,2,0,1:T(2,128)(2,1)S(1)} %copy.14), channel_id=1, replica_groups=mesh['seq'=8,'tensor'=4] {'seq'}, dimensions={1}, use_global_device_ids=true | all-gather | bytes 589824 | tf_op jit(solution)/shard_map/all_gather | solution.py:198
  157.3 5.9 %fusion.2 = f32[2,2,32,1024]{3,2,1,0:T(8,128)} fusion(bf16[2,2048,1024]{2,1,0:T(8,128)(2,1)} %param.13, bf16[2,32,2,2048]{3,2,0,1:T(2,128)(2,1)S(1)} %all_gather.3), kind=kOutput, calls=%fused_computation.2 | convolution fusion | flops 536870912 | bytes 9437184 | tf_op jit(solution)/shard_map/ljgc,lcd->lgjd/dot_general | solution.py:199
  163.2 0.0 reduce-scatter.5.cloned.1.call-update
  163.2 21.4 %reduce-scatter.5.cloned.1.call-done = f32[2,2,8,1024]{3,2,1,0:T(8,128)} async-done(((f32[2,2,32,1024]{3,2,1,0:T(8,128)}), f32[2,2,8,1024]{3,2,1,0:T(8,128)}) %reduce-scatter.5.cloned.1.call-update) | async-done | bytes 131088 | tf_op jit(solution)/shard_map/reduce_scatter | solution.py:200
  184.6 1.5 convert_element_type.15
  (1 shorter events, 0.0 us)
Async XLA Ops:
  6.5 117.3 %all-reduce.3.cloned.1.call-start = ((), (), s32[]{:S(2)}) async-start(), calls=%async_computation.2 | async-start | bytes 2097152
  7.9 2.2 %copy-start = (bf16[2,2,256,2048]{3,2,1,0:T(8,128)(2,1)S(1)}, bf16[2,2,256,2048]{3,2,1,0:T(8,128)(2,1)}, u32[]{:S(2)}) copy-start(bf16[2,2,256,2048]{3,2,1,0:T(8,128)(2,1)} %x_ref.1) | copy-start | bytes 12582916
  10.1 0.9 copy-start.1
  11.1 0.9 copy-start.2
  12.0 0.9 copy-start.3
  43.0 141.6 %reduce-scatter.5.cloned.1.call-start = ((), (), s32[]{:S(2)}) async-start(), calls=%async_computation.1 | async-start | bytes 655360 | tf_op jit(solution)/shard_map/reduce_scatter | solution.py:200
Sparse Core Ops, SparseCore 0:
  43.2 80.6 all-reduce.2
  163.4 21.2 reduce-scatter.4

commit v2 on v1

--- a/solution.py
+++ b/solution.py
@@ -8,6 +8,7 @@
 from jax.experimental.pallas import tpu as pltpu
 from jax.sharding import PartitionSpec as P
 
+MESH = pl.DeviceIdType.MESH
 UNIT = 128
 SUB = 8
 LANE = 128
@@ -42,10 +43,10 @@
         dst[pl.ds(base + k, count, stride=SUB), :] = value[:, k * LANE:(k + 1) * LANE]
 
 
-def local_kernel(granule, bits, info, x_ref, rate_ref, resid_ref, freq_ref, out_ref, xs, pars):
+def local_kernel(granule, bits, info, x_ref, rate_ref, resid_ref, freq_ref, out_ref, xs, pars, acc):
     genomes, span = x_ref.shape[1], x_ref.shape[2]
     modes = rate_ref.shape[1]
-    rows = out_ref.shape[1]
+    rows = acc.shape[1]
     chunk = 32
     first = info[genomes]
     for i, ref in enumerate((rate_ref, resid_ref, freq_ref)):
@@ -62,7 +63,7 @@
             block = jnp.where(src >= 0, block.astype(jnp.float32), 0.0)
             spread_rows(xs.at[g], q * (chunk * SUB), block)
 
-    out_ref[...] = jnp.zeros_like(out_ref)
+    acc[...] = jnp.zeros_like(acc)
     wide = GROUP * SUB
 
     @pl.loop(0, modes // GROUP)
@@ -140,7 +141,7 @@
                     total = now[g * GROUP]
                     for i in range(1, GROUP):
                         total = total + now[g * GROUP + i]
-                    out_ref[0, base + j, g] += total
+                    acc[g, base + j] += total
                 for g in range(genomes):
                     for i in range(GROUP):
                         k = g * GROUP + i
@@ -157,48 +158,167 @@
         wi = tuple(start[g][i][1] for g in range(genomes) for i in range(GROUP))
         lax.fori_loop(0, rows // RUN, row_run, (wr, wi))
 
-
-def local_terms(info, history, rates, residues, freqs, rows, bits, granule):
+    out_ref[0, 0] = acc[...].reshape(out_ref.shape[2:]).astype(out_ref.dtype)
+
+
+def local_terms(info, history, rates, residues, freqs, rows_dev, seq_size, bits, granule):
     layers, genomes, span, chans = history.shape
     modes = rates.shape[1]
     wide = SUB * LANE
+    rows = rows_dev * seq_size
     par_spec = pl.BlockSpec((1, modes, wide), lambda l, c: (l, 0, c))
+    piece = (genomes, seq_size, rows_dev // 2, 2 * SUB, LANE)
     return pl.pallas_call(
         functools.partial(local_kernel, granule, bits),
         grid=(layers, chans // wide),
-        out_shape=jax.ShapeDtypeStruct((layers, rows, genomes, chans // LANE, LANE), jnp.float32),
+        out_shape=jax.ShapeDtypeStruct((layers, chans // wide) + piece, jnp.bfloat16),
         in_specs=[
             pl.BlockSpec(memory_space=pltpu.SMEM),
             pl.BlockSpec((1, genomes, span, wide), lambda l, c: (l, 0, 0, c)),
             par_spec, par_spec, par_spec,
         ],
-        out_specs=pl.BlockSpec((1, rows, genomes, SUB, LANE), lambda l, c: (l, 0, 0, c, 0)),
+        out_specs=pl.BlockSpec((1, 1) + piece, lambda l, c: (l, c, 0, 0, 0, 0, 0)),
         scratch_shapes=[
             pltpu.VMEM((genomes, span * SUB, LANE), jnp.float32),
             pltpu.VMEM((3, modes * SUB, LANE), jnp.float32),
+            pltpu.VMEM((genomes, rows, SUB, LANE), jnp.float32),
         ],
-        compiler_params=pltpu.CompilerParams(vmem_limit_bytes=48 * 1024 * 1024),
+        compiler_params=pltpu.CompilerParams(vmem_limit_bytes=60 * 1024 * 1024),
     )(info, history, rates, residues, freqs)
+
+
+def exchange_kernel(seq, tensor, term, gates, w_hbm, out, w, w_sem, got, flat, full, part, got2, s1, r1, s2, r2, s3, r3):
+    me, tm = lax.axis_index("seq"), lax.axis_index("tensor")
+    layers, blocks, genomes = term.shape[:3]
+    own_rows = gates.shape[0]
+    cols = w.shape[2]
+    barrier = pltpu.get_barrier_semaphore()
+    for k in range(1, seq):
+        pl.semaphore_signal(barrier, inc=1, device_id={"seq": lax.rem(me + k, seq)}, device_id_type=MESH)
+    for k in range(1, tensor):
+        pl.semaphore_signal(barrier, inc=1, device_id={"tensor": lax.rem(tm + k, tensor)}, device_id_type=MESH)
+    fetch = pltpu.make_async_copy(w_hbm, w, w_sem)
+    fetch.start()
+    pl.semaphore_wait(barrier, seq + tensor - 2)
+
+    first = []
+    for k in range(1, seq):
+        peer = lax.rem(me + k, seq)
+        copy = pltpu.make_async_remote_copy(
+            src_ref=term.at[:, :, :, peer], dst_ref=got.at[k], send_sem=s1.at[k], recv_sem=r1.at[k],
+            device_id={"seq": peer}, device_id_type=MESH)
+        copy.start()
+        first.append(copy)
+    flat_shape = (own_rows // layers // genomes * SUB, LANE)
+    for copy in first:
+        copy.wait_recv()
+    for l in range(layers):
+        for c in range(blocks):
+            for g in range(genomes):
+                total = term[l, c, g, me].astype(jnp.float32)
+                for k in range(1, seq):
+                    total = total + got[k, l, c, g].astype(jnp.float32)
+                flat[c, pl.ds((l * genomes + g) * flat_shape[0], flat_shape[0]), :] = total.reshape(flat_shape)
+    for c in range(blocks):
+        for k in range(SUB):
+            at = pl.ds((c * SUB + k) * LANE, LANE)
+            value = flat[c, pl.ds(k, own_rows, stride=SUB), :] * gates[:, at].astype(jnp.float32)
+            full[me, :, at] = value.astype(full.dtype)
+
+    second = []
+    for k in range(1, seq):
+        copy = pltpu.make_async_remote_copy(
+            src_ref=full.at[me], dst_ref=full.at[me], send_sem=s2.at[k], recv_sem=r2.at[k],
+            device_id={"seq": lax.rem(me + k, seq)}, device_id_type=MESH)
+        copy.start()
+        second.append(copy)
+    fetch.wait()
+    for k in range(1, seq):
+        src = lax.rem(me - k + seq, seq)
+        pltpu.make_async_remote_copy(
+            src_ref=full.at[src], dst_ref=full.at[src], send_sem=s2.at[k], recv_sem=r2.at[k],
+            device_id={"seq": lax.rem(me + k, seq)}, device_id_type=MESH).wait_recv()
+
+    share = seq // tensor
+    wide = part.shape[3]
+    per = tensor if seq * own_rows <= 256 else 1
+    third = []
+    for n in range(cols // wide):
+        @pl.loop(0, tensor // per)
+        def _(t):
+            block = full[pl.ds(t * (per * share), per * share)].reshape(per * share * own_rows, full.shape[2])
+            both = [jnp.dot(block, w[l, :, n * wide:(n + 1) * wide], preferred_element_type=jnp.float32)
+                    for l in range(layers)]
+            at = lax.broadcasted_iota(jnp.int32, both[0].shape, 0)
+            owner = lax.rem(at, own_rows) // (own_rows // layers)
+            value = both[0]
+            for l in range(1, layers):
+                value = jnp.where(owner == l, both[l], value)
+            part[n, pl.ds(t * per, per)] = value.reshape(per, share * own_rows, wide)
+        for k in range(1, tensor):
+            peer = lax.rem(tm + k, tensor)
+            copy = pltpu.make_async_remote_copy(
+                src_ref=part.at[n, peer], dst_ref=got2.at[n, k], send_sem=s3.at[n, k], recv_sem=r3.at[n, k],
+                device_id={"tensor": peer}, device_id_type=MESH)
+            copy.start()
+            third.append(copy)
+    for n in range(cols // wide):
+        total = part[n, tm]
+        for k in range(1, tensor):
+            third[n * (tensor - 1) + k - 1].wait_recv()
+            total = total + got2[n, k]
+        out[:, n * wide:(n + 1) * wide] = total.astype(out.dtype)
+    for copy in first + second + third:
+        copy.wait_send()
+
+
+def exchange(term, gates, w_out, seq, tensor):
+    own_rows, chans = gates.shape
+    layers, _, cols = w_out.shape
+    wide = min(cols, 256)
+    share = seq // tensor
+    vmem = pl.BlockSpec(memory_space=pltpu.VMEM)
+    return pl.pallas_call(
+        functools.partial(exchange_kernel, seq, tensor),
+        out_shape=jax.ShapeDtypeStruct((share * own_rows, cols), jnp.bfloat16),
+        in_specs=[vmem, vmem, pl.BlockSpec(memory_space=pl.ANY)],
+        out_specs=vmem,
+        scratch_shapes=[
+            pltpu.VMEM(w_out.shape, w_out.dtype),
+            pltpu.SemaphoreType.DMA,
+            pltpu.VMEM((seq,) + term.shape[:3] + term.shape[4:], term.dtype),
+            pltpu.VMEM((term.shape[1], own_rows * SUB, LANE), jnp.float32),
+            pltpu.VMEM((seq, own_rows, chans), jnp.bfloat16),
+            pltpu.VMEM((cols // wide, tensor, share * own_rows, wide), jnp.float32),
+            pltpu.VMEM((cols // wide, tensor, share * own_rows, wide), jnp.float32),
+            pltpu.SemaphoreType.DMA((seq,)),
+            pltpu.SemaphoreType.DMA((seq,)),
+            pltpu.SemaphoreType.DMA((seq,)),
+            pltpu.SemaphoreType.DMA((seq,)),
+            pltpu.SemaphoreType.DMA((cols // wide, tensor)),
+            pltpu.SemaphoreType.DMA((cols // wide, tensor)),
+        ],
+        compiler_params=pltpu.CompilerParams(
+            collective_id=0, has_side_effects=True, vmem_limit_bytes=60 * 1024 * 1024),
+    )(term, gates, w_out)
 
 
 def shards(history, gates, rates, residues, freqs, w_out, lengths, tile_index):
     layers, genomes, span, chans = history.shape
     rows_dev = gates.shape[2]
-    seq_size = lax.axis_size("seq")
+    seq_size, tensor_size = lax.axis_size("seq"), lax.axis_size("tensor")
     tile = rows_dev * seq_size
     granule = math.gcd(UNIT, tile)
     bits = (span * seq_size // granule).bit_length()
     flush_at = lengths + tile * tile_index[0]
     first = lax.axis_index("seq") * span
     info = jnp.concatenate([flush_at, first[None]]).astype(jnp.int32)
-    term = local_terms(info, history, rates, residues, freqs, tile, bits, granule)
-    summed = lax.psum_scatter(term, "seq", scatter_dimension=1, tiled=True)
-    gates_t = gates.transpose(0, 2, 1, 3).astype(jnp.float32)
-    gated = (summed.reshape(layers, rows_dev, genomes, chans) * gates_t).astype(jnp.bfloat16)
-    full = lax.all_gather(gated, "seq", axis=1, tiled=True)
-    partial_out = jnp.einsum("ljgc,lcd->lgjd", full, w_out, preferred_element_type=jnp.float32)
-    mixed = lax.psum_scatter(partial_out, "tensor", scatter_dimension=2, tiled=True)
-    return mixed.astype(jnp.bfloat16)
+    term = local_terms(info, history, rates, residues, freqs, rows_dev, seq_size, bits, granule)
+    own_rows = layers * genomes * rows_dev
+    mixed = exchange(term, gates.reshape(own_rows, chans), w_out, seq_size, tensor_size)
+    share = seq_size // tensor_size
+    mixed = mixed.reshape(share, layers, genomes, rows_dev, -1).transpose(1, 2, 0, 3, 4)
+    return mixed.reshape(layers, genomes, share * rows_dev, -1)
 
 
 def solution(mesh):

time: 193 us -> 75.8 us (0.39)
  the two profiles are of different devices: /device:TPU:0 before, /device:TPU:27 now
where the time goes in v2:
time: 75.8 us; the launch traced here: 75.6 us
  Pallas kernels  70.5 us (93%)
  local copies, waits for them, and re-layouts  3.04 us (4%)
  other arithmetic  1.33 us (2%)
    pallas_call x1, Pallas kernels, exchange(): pl.pallas_call(functools.partial(exchange_kernel, seq, tensor), out_shape...  40.1 us
    pallas_call x1, Pallas kernels, local_terms(): pl.pallas_call(functools.partial(local_kernel, granule, bits), grid=(laye...  30.5 us

profile of v2, /device:TPU:27, one launch (start us, length us, event | category | flops | bytes accessed | tf_op | source)
XLA Modules:
  0.0 75.6 jit_solution(3963984719684692761)
XLA Ops:
  0.7 0.7 broadcast_add_fusion
  1.3 0.7 pad_add_fusion.info
  2.0 1.5 %reshape.11.gates = bf16[16,2048]{1,0:T(8,128)(2,1)} reshape(bf16[2,2,4,2048]{3,2,1,0:T(4,128)(2,1)} %param.9) | data formatting | bytes 131072 | tf_op jit(solution)/shard_map/reshape | solution.py:318
  3.5 30.5 %shard_map.82.term = bf16[2,2,2,8,2,16,128]{6,5,4,3,2,1,0:T(8,128)(2,1)} custom-call(s32[3]{0:T(128)} %pad_add_fusion.info, bf16[2,2,256,2048]{3,2,1,0:T(8,128)(2,1)} %x_ref.1, f32[2,16,2048]{2,1,0:T(8,128)} %rate_ref.1, f32[2,16,2048]{2,1,0:T(8,128)} %resid_ref.1, f32[2,16,2048]{2,1,0:T(8,128)} %freq_ref.1), custom_call_target="tpu_custom_call" | custom-call | tf_op jit(solution)/shard_map/pallas_call | solution.py:171
  33.9 40.1 %shard_map.83 = bf16[32,1024]{1,0:T(8,128)(2,1)} custom-call(bf16[2,2,2,8,2,16,128]{6,5,4,3,2,1,0:T(8,128)(2,1)} %shard_map.82.term, bf16[16,2048]{1,0:T(8,128)(2,1)} %reshape.11.gates, bf16[2,2048,1024]{2,1,0:T(8,128)(2,1)} %w_hbm.1), custom_call_target="tpu_custom_call" | custom-call | tf_op jit(solution)/shard_map/pallas_call | solution.py:281
  74.0 0.9 %reshape.12 = bf16[2,2,2,4,1024]{4,3,2,1,0:T(4,128)(2,1)S(1)} reshape(bf16[32,1024]{1,0:T(8,128)(2,1)} %shard_map.83) | data formatting | bytes 131072 | tf_op jit(solution)/shard_map/reshape | solution.py:320
  74.9 0.6 reshape.13
  (1 shorter events, 0.0 us)

commit v3 on v1

v3 whole, which is shorter than its diff:
```python
import functools
import math

import jax
import jax.numpy as jnp
from jax import lax
from jax.experimental import pallas as pl
from jax.experimental.pallas import tpu as pltpu
from jax.sharding import PartitionSpec as P

MESH = pl.DeviceIdType.MESH
UNIT = 128
SUB = 8
LANE = 128
GROUP = 4
STEPS = 32
RUN = 32


def cmul(ar, ai, br, bi):
    return ar * br - ai * bi, ar * bi + ai * br


def csq(ar, ai):
    return ar * ar - ai * ai, 2.0 * (ar * ai)


def cos_sin(angle):
    y = (angle - 1.57079637050628662) + 4.37113883e-8
    y2 = y * y
    s = jnp.full_like(y, 1.0 / math.factorial(13))
    for n, sign in ((11, -1), (9, 1), (7, -1), (5, 1), (3, -1), (1, 1)):
        s = s * y2 + sign / math.factorial(n)
    c = jnp.full_like(y, -1.0 / math.factorial(14))
    for n, sign in ((12, 1), (10, -1), (8, 1), (6, -1), (4, 1), (2, -1), (0, 1)):
        c = c * y2 + sign / math.factorial(n)
    return -(s * y), c


def spread_rows(dst, base, value):
    count = value.shape[0]
    for k in range(SUB):
        dst[pl.ds(base + k, count, stride=SUB), :] = value[:, k * LANE:(k + 1) * LANE]


def local_step(granule, bits, first, starts, x_ref, params, l, c, acc, xs, pars):
    genomes, span = x_ref.shape[:2]
    modes = params[0].shape[1]
    rows = acc.shape[1]
    chunk = 32
    wide_cols = SUB * LANE
    for i, ref in enumerate(params):
        spread_rows(pars.at[i], 0, ref[l, :, pl.ds(pl.multiple_of(c * wide_cols, wide_cols), wide_cols)])
    hops, blocks_live = [], []
    for g in range(genomes):
        ahead = jnp.full((SUB, LANE), starts[g] - first, jnp.int32)
        live = jnp.minimum(jnp.maximum(ahead, 0), span)
        blocks_live.append(live)
        hops.append(jnp.maximum(ahead - live, 0))

        @pl.loop(0, span // chunk)
        def _(q):
            block = x_ref[g, pl.ds(pl.multiple_of(q * chunk, chunk), chunk), :]
            spread_rows(xs.at[g], q * (chunk * SUB), block.astype(jnp.float32))

    acc[...] = jnp.zeros_like(acc)
    wide = GROUP * SUB

    @pl.loop(0, modes // GROUP)
    def _(mg):
        at = pl.ds(pl.multiple_of(mg * wide, wide), wide)
        rate, resid, freq = pars[0, at, :], pars[1, at, :], pars[2, at, :]
        decay = jnp.exp(-rate)
        c, s = cos_sin(freq)
        zr, zi = decay * c, decay * s
        trace, norm = 2.0 * zr, zr * zr + zi * zi
        amp = resid * jnp.sqrt(rate)

        def cut(v):
            return [v[i * SUB:(i + 1) * SUB] for i in range(GROUP)]

        zr_c, zi_c, tr_c, no_c = cut(zr), cut(zi), cut(trace), cut(norm)
        pr, pi = zr, zi
        for _ in range(int(math.log2(STEPS))):
            pr, pi = csq(pr, pi)
        br_c, bi_c = cut(pr), cut(pi)
        n_state = genomes * GROUP
        zero = jnp.zeros((SUB, LANE), jnp.float32)

        def block_step(blk, carry):
            re, im = carry
            a = [zero] * n_state
            b = [zero] * n_state
            for t in range(STEPS):
                for g in range(genomes):
                    x = xs[g, pl.ds(pl.multiple_of(blk * (STEPS * SUB) + t * SUB, SUB), SUB), :]
                    for i in range(GROUP):
                        k = g * GROUP + i
                        a[k], b[k] = b[k] + tr_c[i] * a[k], x - no_c[i] * a[k]
            new_re, new_im = [], []
            for g in range(genomes):
                for i in range(GROUP):
                    k = g * GROUP + i
                    sr, si = cmul(br_c[i], bi_c[i], re[k], im[k])
                    keep = blocks_live[g] > blk * STEPS
                    new_re.append(jnp.where(keep, sr + (zr_c[i] * a[k] + b[k]), re[k]))
                    new_im.append(jnp.where(keep, si + zi_c[i] * a[k], im[k]))
            return tuple(new_re), tuple(new_im)

        init = ((zero,) * n_state, (zero,) * n_state)
        re, im = lax.fori_loop(0, span // STEPS, block_step, init)

        pr, pi = zr, zi
        for _ in range(int(math.log2(granule))):
            pr, pi = csq(pr, pi)
        lead_r, lead_i = amp * zr, amp * zi
        far_r = [cut(lead_r) for _ in range(genomes)]
        far_i = [cut(lead_i) for _ in range(genomes)]
        for bit in range(bits):
            pr_c, pi_c = cut(pr), cut(pi)
            for g in range(genomes):
                on = (hops[g] & (granule << bit)) != 0
                for i in range(GROUP):
                    nr, ni = cmul(far_r[g][i], far_i[g][i], pr_c[i], pi_c[i])
                    far_r[g][i] = jnp.where(on, nr, far_r[g][i])
                    far_i[g][i] = jnp.where(on, ni, far_i[g][i])
            if bit + 1 < bits:
                pr, pi = csq(pr, pi)
        start = []
        for g in range(genomes):
            fr, fi = far_r[g], far_i[g]
            start.append([cmul(re[g * GROUP + i], im[g * GROUP + i], fr[i], fi[i]) for i in range(GROUP)])
        qr, qi = zr, zi
        for _ in range(int(math.log2(RUN))):
            qr, qi = csq(qr, qi)
        qr_c, qi_c = cut(qr), cut(qi)

        def row_run(run, carry):
            wr, wi = carry
            base = run * RUN
            old = [None] * n_state
            now = list(wr)
            for j in range(RUN):
                for g in range(genomes):
                    total = now[g * GROUP]
                    for i in range(1, GROUP):
                        total = total + now[g * GROUP + i]
                    acc[g, base + j] += total
                for g in range(genomes):
                    for i in range(GROUP):
                        k = g * GROUP + i
                        if j == 0:
                            nxt = wr[k] * zr_c[i] - wi[k] * zi_c[i]
                        else:
                            nxt = tr_c[i] * now[k] - no_c[i] * old[k]
                        old[k], now[k] = now[k], nxt
            moved = [cmul(wr[g * GROUP + i], wi[g * GROUP + i], qr_c[i], qi_c[i])
                     for g in range(genomes) for i in range(GROUP)]
            return tuple(m[0] for m in moved), tuple(m[1] for m in moved)

        wr = tuple(start[g][i][0] for g in range(genomes) for i in range(GROUP))
        wi = tuple(start[g][i][1] for g in range(genomes) for i in range(GROUP))
        lax.fori_loop(0, rows // RUN, row_run, (wr, wi))


def kernel(seq, tensor, granule, bits, lengths, tile_index, rates, residues, freqs, gates, hist_hbm, w_hbm, out,
           hist, h_sem, w, w_sem, xs, pars, acc, term, got, flat, scale, full, part, got2, final,
           s1, r1, s2, r2, s3, r3):
    me, tm = lax.axis_index("seq"), lax.axis_index("tensor")
    blocks, layers, genomes = term.shape[:3]
    rows_dev = gates.shape[2]
    own_rows = layers * genomes * rows_dev
    cols = w.shape[2]
    wide_cols = SUB * LANE
    barrier = pltpu.get_barrier_semaphore()
    for k in range(1, seq):
        pl.semaphore_signal(barrier, inc=1, device_id={"seq": lax.rem(me + k, seq)}, device_id_type=MESH)
    for k in range(1, tensor):
        pl.semaphore_signal(barrier, inc=1, device_id={"tensor": lax.rem(tm + k, tensor)}, device_id_type=MESH)

    def load(c, l):
        return pltpu.make_async_copy(
            hist_hbm.at[l, :, :, pl.ds(pl.multiple_of(c * wide_cols, wide_cols), wide_cols)],
            hist.at[c, l], h_sem.at[c, l])

    for c in range(blocks):
        for l in range(layers):
            load(c, l).start()
    fetch = pltpu.make_async_copy(w_hbm, w, w_sem)
    fetch.start()
    tile = rows_dev * seq
    starts = [lengths[g] + tile * tile_index[0] for g in range(genomes)]
    first = me * hist.shape[3]
    for l in range(layers):
        for g in range(genomes):
            scale[pl.ds((l * genomes + g) * rows_dev, rows_dev), :] = gates[l, g].astype(jnp.float32)

    def rows_out(c, l, k):
        peer = lax.rem(me + k, seq)
        return pltpu.make_async_remote_copy(
            src_ref=term.at[c, l, :, peer], dst_ref=got.at[c, l, k],
            send_sem=s1.at[c, l, k], recv_sem=r1.at[c, l, k],
            device_id={"seq": peer}, device_id_type=MESH)

    def gated_out(c, k, src):
        return pltpu.make_async_remote_copy(
            src_ref=full.at[c, src], dst_ref=full.at[c, src], send_sem=s2.at[c, k], recv_sem=r2.at[c, k],
            device_id={"seq": lax.rem(me + k, seq)}, device_id_type=MESH)

    def gate(c):
        count = rows_dev * SUB
        for l in range(layers):
            for k in range(1, seq):
                rows_out(c, l, k).wait_recv()
            for g in range(genomes):
                total = term[c, l, g, me].astype(jnp.float32)
                for k in range(1, seq):
                    total = total + got[c, l, k, g].astype(jnp.float32)
                flat[pl.ds((l * genomes + g) * count, count), :] = total.reshape(count, LANE)
        for k in range(SUB):
            value = flat[pl.ds(k, own_rows, stride=SUB), :] * scale[:, pl.ds((c * SUB + k) * LANE, LANE)]
            full[c, me, :, pl.ds(k * LANE, LANE)] = value.astype(full.dtype)
        for k in range(1, seq):
            gated_out(c, k, me).start()

    @pl.loop(0, blocks * layers)
    def _(step):
        c, l = step // layers, step % layers
        load(c, l).wait()
        local_step(granule, bits, first, starts, hist.at[c, l], (rates, residues, freqs), l, c, acc, xs, pars)
        term[c, l] = acc[...].reshape(term.shape[2:]).astype(term.dtype)

        @pl.when(step == 0)
        def _():
            pl.semaphore_wait(barrier, seq + tensor - 2)

        for k in range(1, seq):
            rows_out(c, l, k).start()
        for done in range(blocks - 1):
            @pl.when(step == (done + 1) * layers)
            def _():
                gate(done)

    fetch.wait()
    share = seq // tensor
    wide = part.shape[3]
    per = tensor if seq * own_rows <= 256 else 1

    def project(c, n):
        @pl.loop(0, tensor // per)
        def _(t):
            block = full[c, pl.ds(t * (per * share), per * share)].reshape(per * share * own_rows, wide_cols)
            both = [jnp.dot(block, w[l, pl.ds(c * wide_cols, wide_cols), n * wide:(n + 1) * wide],
                            preferred_element_type=jnp.float32) for l in range(layers)]
            at = lax.broadcasted_iota(jnp.int32, both[0].shape, 0)
            owner = lax.rem(at, own_rows) // (own_rows // layers)
            value = both[0]
            for l in range(1, layers):
                value = jnp.where(owner == l, both[l], value)
            value = value.reshape(per, share * own_rows, wide)
            where = pl.ds(t * per, per)
            part[n, where] = value if c == 0 else part[n, where] + value

    def gathered(c):
        for k in range(1, seq):
            gated_out(c, k, lax.rem(me - k + seq, seq)).wait_recv()

    def shares_out(n, k):
        peer = lax.rem(tm + k, tensor)
        return pltpu.make_async_remote_copy(
            src_ref=part.at[n, peer], dst_ref=got2.at[n, k], send_sem=s3.at[n, k], recv_sem=r3.at[n, k],
            device_id={"tensor": peer}, device_id_type=MESH)

    chunks = cols // wide
    for c in range(blocks - 1):
        gathered(c)
        for n in range(chunks):
            project(c, n)
    gate(blocks - 1)
    gathered(blocks - 1)
    for n in range(chunks):
        project(blocks - 1, n)
        for k in range(1, tensor):
            shares_out(n, k).start()
    for n in range(chunks):
        total = part[n, tm]
        for k in range(1, tensor):
            shares_out(n, k).wait_recv()
            total = total + got2[n, k]
        for o in range(share):
            for l in range(layers):
                for g in range(genomes):
                    at = o * own_rows + (l * genomes + g) * rows_dev
                    final[l, g, o * rows_dev:(o + 1) * rows_dev, n * wide:(n + 1) * wide] = total[at:at + rows_dev]
    out[...] = final[...].astype(out.dtype)
    for k in range(1, seq):
        for c in range(blocks):
            for l in range(layers):
                rows_out(c, l, k).wait_send()
            gated_out(c, k, me).wait_send()
    for k in range(1, tensor):
        for n in range(chunks):
            shares_out(n, k).wait_send()


def shards(history, gates, rates, residues, freqs, w_out, lengths, tile_index):
    layers, genomes, span, chans = history.shape
    rows_dev = gates.shape[2]
    seq, tensor = lax.axis_size("seq"), lax.axis_size("tensor")
    tile = rows_dev * seq
    granule = math.gcd(UNIT, tile)
    bits = (span * seq // granule).bit_length()
    modes = rates.shape[1]
    wide_cols = SUB * LANE
    blocks = chans // wide_cols
    own_rows = layers * genomes * rows_dev
    cols = w_out.shape[2]
    wide = min(cols, 256)
    share = seq // tensor
    vmem = pl.BlockSpec(memory_space=pltpu.VMEM)
    smem = pl.BlockSpec(memory_space=pltpu.SMEM)
    hbm = pl.BlockSpec(memory_space=pl.ANY)
    piece = (rows_dev // 2, 2 * SUB, LANE)
    dma = pltpu.SemaphoreType.DMA
    return pl.pallas_call(
        functools.partial(kernel, seq, tensor, granule, bits),
        out_shape=jax.ShapeDtypeStruct((layers, genomes, share * rows_dev, cols), jnp.bfloat16),
        in_specs=[smem, smem, vmem, vmem, vmem, vmem, hbm, hbm],
        out_specs=vmem,
        scratch_shapes=[
            pltpu.VMEM((blocks, layers, genomes, span, wide_cols), history.dtype),
            dma((blocks, layers)),
            pltpu.VMEM(w_out.shape, w_out.dtype),
            dma,
            pltpu.VMEM((genomes, span * SUB, LANE), jnp.float32),
            pltpu.VMEM((3, modes * SUB, LANE), jnp.float32),
            pltpu.VMEM((genomes, tile, SUB, LANE), jnp.float32),
            pltpu.VMEM((blocks, layers, genomes, seq) + piece, jnp.bfloat16),
            pltpu.VMEM((blocks, layers, seq, genomes) + piece, jnp.bfloat16),
            pltpu.VMEM((own_rows * SUB, LANE), jnp.float32),
            pltpu.VMEM((own_rows, chans), jnp.float32),
            pltpu.VMEM((blocks, seq, own_rows, wide_cols), jnp.bfloat16),
            pltpu.VMEM((cols // wide, tensor, share * own_rows, wide), jnp.float32),
            pltpu.VMEM((cols // wide, tensor, share * own_rows, wide), jnp.float32),
            pltpu.VMEM((layers, genomes, share * rows_dev, cols), jnp.float32),
            dma((blocks, layers, seq)), dma((blocks, layers, seq)),
            dma((blocks, seq)), dma((blocks, seq)),
            dma((cols // wide, tensor)), dma((cols // wide, tensor)),
        ],
        compiler_params=pltpu.CompilerParams(
            collective_id=0, has_side_effects=True, vmem_limit_bytes=60 * 1024 * 1024),
    )(lengths, tile_index, rates, residues, freqs, gates, history, w_out)


def solution(mesh):
    in_specs = (
        P(None, None, "seq", "tensor"),
        P(None, None, "seq", "tensor"),
        P(None, None, "tensor"),
        P(None, None, "tensor"),
        P(None, None, "tensor"),
        P(None, "tensor", "seq"),
        P(),
        P(),
    )
    out_specs = P(None, None, "tensor", "seq")
    return jax.shard_map(shards, mesh=mesh, in_specs=in_specs, out_specs=out_specs, check_vma=False)
```

time: 193 us -> 57.1 us (0.30)
  waiting for transfers between devices: 100 us -> 0 us
  blocking collectives: 31.4 us -> 0 us
  Pallas kernels: 30 us -> 53.9 us
  between operations: 14.7 us -> 0.66 us
  matrix products: 5.9 us -> 0 us
  local copies, waits for them, and re-layouts: 7.33 us -> 1.47 us
  other arithmetic: 3.23 us -> 0 us
    unnamed x3 -> x0, waiting for transfers between devices: 78.9 us -> none
    all_gather x1 -> x0, blocking collectives: 31.4 us -> none  [shards(): full = lax.all_gather(gated, 'seq', axis=1, tiled=True)]
    pallas_call x1, Pallas kernels: 30 us -> 53.9 us  [shards(): pl.pallas_call(functools.partial(kernel, seq, tensor, granule, bits), out...]
    reduce_scatter x1 -> x0, waiting for transfers between devices: 21.4 us -> none  [shards(): lax.psum_scatter(partial_out, 'tensor', scatter_dimension=2, tiled=True)]
    dot_general x1 -> x0, matrix products: 5.9 us -> none  [shards(): jnp.einsum('ljgc,lcd->lgjd', full, w_out, preferred_element_type=jnp.floa...]
    unnamed x10 -> x1, local copies, waits for them, and re-layouts: 7.19 us -> 1.47 us
    convert_element_type x2 -> x0, other arithmetic: 2.49 us -> none  [the longest x1 1.54 us: shards(): return mixed.astype(jnp.bfloat16)]
  transfers between devices with their start and end apart: 2 -> 0, of which waited for: 2 -> 0; matrix products, arithmetic and copies ran while one was open for 1% -> 0% of each run, Pallas kernels for 0% -> 0%
where the time goes in v3:
time: 57.1 us; the launch traced here: 56 us
  Pallas kernels  53.9 us (94%)
  local copies, waits for them, and re-layouts  1.47 us (3%)
  between operations  0.66 us (1%)
    pallas_call x1, Pallas kernels, shards(): pl.pallas_call(functools.partial(kernel, seq, tensor, granule, bits), out...  53.9 us
    unnamed x1, local copies, waits for them, and re-layouts  1.47 us

profile of v3, /device:TPU:0, one launch (start us, length us, event | category | flops | bytes accessed | tf_op | source)
XLA Modules:
  0.0 56.0 jit_solution(8739900030917471534)
XLA Ops:
  0.7 53.9 %shard_map.82 = bf16[2,2,8,1024]{3,2,1,0:T(8,128)(2,1)} custom-call(s32[2]{0:T(128)} %lengths.1, s32[1]{0:T(128)S(6)} %copy.10.tile_index, f32[2,16,2048]{2,1,0:T(8,128)} %rates.1, f32[2,16,2048]{2,1,0:T(8,128)} %residues.1, f32[2,16,2048]{2,1,0:T(8,128)} %freqs.1, bf16[2,2,4,2048]{3,2,1,0:T(4,128)(2,1)} %gates.1, bf16[2,2,256,2048]{3,2,1,0:T(8,128)(2,1)} %hist_hbm.1, ...), custom_call_target="tpu_custom_call" | custom-call | tf_op jit(solution)/shard_map/pallas_call | solution.py:325
  54.5 1.5 %copy.11 = bf16[2,2,8,1024]{3,2,1,0:T(8,128)(2,1)} copy(bf16[2,2,8,1024]{3,2,1,0:T(8,128)(2,1)} %shard_map.82) | data formatting | bytes 131072

commit v4 on v3

--- a/solution.py
+++ b/solution.py
@@ -164,7 +164,7 @@
 
 
 def kernel(seq, tensor, granule, bits, lengths, tile_index, rates, residues, freqs, gates, hist_hbm, w_hbm, out,
-           hist, h_sem, w, w_sem, xs, pars, acc, term, got, flat, scale, full, part, got2, final,
+           hist, h_sem, w, w_sem, xs, pars, acc, term, got, flat, folded, scale, full, part, got2, final,
            s1, r1, s2, r2, s3, r3):
     me, tm = lax.axis_index("seq"), lax.axis_index("tensor")
     blocks, layers, genomes = term.shape[:3]
@@ -202,26 +202,32 @@
             send_sem=s1.at[c, l, k], recv_sem=r1.at[c, l, k],
             device_id={"seq": peer}, device_id_type=MESH)
 
-    def gated_out(c, k, src):
+    def gated_out(c, l, k, src):
         return pltpu.make_async_remote_copy(
-            src_ref=full.at[c, src], dst_ref=full.at[c, src], send_sem=s2.at[c, k], recv_sem=r2.at[c, k],
+            src_ref=full.at[c, l, src], dst_ref=full.at[c, l, src],
+            send_sem=s2.at[c, l, k], recv_sem=r2.at[c, l, k],
             device_id={"seq": lax.rem(me + k, seq)}, device_id_type=MESH)
 
-    def gate(c):
+    layer_rows = genomes * rows_dev
+    fold = SUB // 2
+
+    def gate(c, l):
         count = rows_dev * SUB
-        for l in range(layers):
+        for k in range(1, seq):
+            rows_out(c, l, k).wait_recv()
+        for g in range(genomes):
+            total = term[c, l, g, me].astype(jnp.float32)
             for k in range(1, seq):
-                rows_out(c, l, k).wait_recv()
-            for g in range(genomes):
-                total = term[c, l, g, me].astype(jnp.float32)
-                for k in range(1, seq):
-                    total = total + got[c, l, k, g].astype(jnp.float32)
-                flat[pl.ds((l * genomes + g) * count, count), :] = total.reshape(count, LANE)
+                total = total + got[c, l, k, g].astype(jnp.float32)
+            flat[pl.ds(g * count, count), :] = total.reshape(count, LANE)
         for k in range(SUB):
-            value = flat[pl.ds(k, own_rows, stride=SUB), :] * scale[:, pl.ds((c * SUB + k) * LANE, LANE)]
-            full[c, me, :, pl.ds(k * LANE, LANE)] = value.astype(full.dtype)
-        for k in range(1, seq):
-            gated_out(c, k, me).start()
+            at = pl.ds(pl.multiple_of(l * layer_rows, layer_rows), layer_rows)
+            lanes = pl.ds(pl.multiple_of((c * SUB + k) * LANE, LANE), LANE)
+            value = flat[pl.ds(k, layer_rows, stride=SUB), :] * scale[at, lanes]
+            folded[pl.ds(k // fold * layer_rows, layer_rows), pl.ds(k % fold * LANE, LANE)] = value
+        full[c, l, me] = folded[...].astype(full.dtype)
+        for k in range(1, seq):
+            gated_out(c, l, k, me).start()
 
     @pl.loop(0, blocks * layers)
     def _(step):
@@ -236,71 +242,75 @@
 
         for k in range(1, seq):
             rows_out(c, l, k).start()
-        for done in range(blocks - 1):
-            @pl.when(step == (done + 1) * layers)
-            def _():
-                gate(done)
+
+        @pl.when(step > 0)
+        def _():
+            gate((step - 1) // layers, (step - 1) % layers)
 
     fetch.wait()
     share = seq // tensor
-    wide = part.shape[3]
-    per = tensor if seq * own_rows <= 256 else 1
-
-    def project(c, n):
+    wide = part.shape[4]
+    per = tensor if 2 * seq * layer_rows <= 256 else 1
+    depth = fold * LANE
+
+    def project(c, l, n):
         @pl.loop(0, tensor // per)
         def _(t):
-            block = full[c, pl.ds(t * (per * share), per * share)].reshape(per * share * own_rows, wide_cols)
-            both = [jnp.dot(block, w[l, pl.ds(c * wide_cols, wide_cols), n * wide:(n + 1) * wide],
-                            preferred_element_type=jnp.float32) for l in range(layers)]
-            at = lax.broadcasted_iota(jnp.int32, both[0].shape, 0)
-            owner = lax.rem(at, own_rows) // (own_rows // layers)
-            value = both[0]
-            for l in range(1, layers):
-                value = jnp.where(owner == l, both[l], value)
-            value = value.reshape(per, share * own_rows, wide)
+            block = full[c, l, pl.ds(t * (per * share), per * share)].reshape(per * share * 2 * layer_rows, depth)
+            value = 0.0
+            for h in range(2):
+                both = jnp.dot(block, w[l, pl.ds(c * wide_cols + h * depth, depth), n * wide:(n + 1) * wide],
+                               preferred_element_type=jnp.float32)
+                value = value + both.reshape(per * share, 2, layer_rows, wide)[:, h]
+            value = value.reshape(per, share * layer_rows, wide)
             where = pl.ds(t * per, per)
-            part[n, where] = value if c == 0 else part[n, where] + value
-
-    def gathered(c):
-        for k in range(1, seq):
-            gated_out(c, k, lax.rem(me - k + seq, seq)).wait_recv()
-
-    def shares_out(n, k):
+            part[l, n, where] = value if c == 0 else part[l, n, where] + value
+
+    def gathered(c, l):
+        for k in range(1, seq):
+            gated_out(c, l, k, lax.rem(me - k + seq, seq)).wait_recv()
+
+    def shares_out(l, n, k):
         peer = lax.rem(tm + k, tensor)
         return pltpu.make_async_remote_copy(
-            src_ref=part.at[n, peer], dst_ref=got2.at[n, k], send_sem=s3.at[n, k], recv_sem=r3.at[n, k],
+            src_ref=part.at[l, n, peer], dst_ref=got2.at[l, n, k], send_sem=s3.at[l, n, k], recv_sem=r3.at[l, n, k],
             device_id={"tensor": peer}, device_id_type=MESH)
 
     chunks = cols // wide
-    for c in range(blocks - 1):
-        gathered(c)
+    order = [(c, l) for c in range(blocks) for l in range(layers)]
+
+    def advance(c, l):
+        gathered(c, l)
         for n in range(chunks):
-            project(c, n)
-    gate(blocks - 1)
-    gathered(blocks - 1)
-    for n in range(chunks):
-        project(blocks - 1, n)
-        for k in range(1, tensor):
-            shares_out(n, k).start()
-    for n in range(chunks):
-        total = part[n, tm]
-        for k in range(1, tensor):
-            shares_out(n, k).wait_recv()
-            total = total + got2[n, k]
-        for o in range(share):
-            for l in range(layers):
+            project(c, l, n)
+            if c == blocks - 1:
+                for k in range(1, tensor):
+                    shares_out(l, n, k).start()
+
+    for c, l in order[:-2]:
+        advance(c, l)
+    gate(*order[-1])
+    for c, l in order[-2:]:
+        advance(c, l)
+    for l in range(layers):
+        for n in range(chunks):
+            total = part[l, n, tm]
+            for k in range(1, tensor):
+                shares_out(l, n, k).wait_recv()
+                total = total + got2[l, n, k]
+            for o in range(share):
                 for g in range(genomes):
-                    at = o * own_rows + (l * genomes + g) * rows_dev
+                    at = o * layer_rows + g * rows_dev
                     final[l, g, o * rows_dev:(o + 1) * rows_dev, n * wide:(n + 1) * wide] = total[at:at + rows_dev]
     out[...] = final[...].astype(out.dtype)
-    for k in range(1, seq):
-        for c in range(blocks):
-            for l in range(layers):
-                rows_out(c, l, k).wait_send()
-            gated_out(c, k, me).wait_send()
-    for k in range(1, tensor):
+    for c, l in order:
+        for k in range(1, seq):
+            rows_out(c, l, k).wait_send()
+            gated_out(c, l, k, me).wait_send()
+    for l in range(layers):
         for n in range(chunks):
-            shares_out(n, k).wait_send()
+            for k in range(1, tensor):
+                shares_out(l, n, k).wait_send()
 
 
 def shards(history, gates, rates, residues, freqs, w_out, lengths, tile_index):
@@ -337,15 +347,16 @@
             pltpu.VMEM((genomes, tile, SUB, LANE), jnp.float32),
             pltpu.VMEM((blocks, layers, genomes, seq) + piece, jnp.bfloat16),
             pltpu.VMEM((blocks, layers, seq, genomes) + piece, jnp.bfloat16),
-            pltpu.VMEM((own_rows * SUB, LANE), jnp.float32),
+            pltpu.VMEM((genomes * rows_dev * SUB, LANE), jnp.float32),
+            pltpu.VMEM((2 * genomes * rows_dev, wide_cols // 2), jnp.float32),
             pltpu.VMEM((own_rows, chans), jnp.float32),
-            pltpu.VMEM((blocks, seq, own_rows, wide_cols), jnp.bfloat16),
-            pltpu.VMEM((cols // wide, tensor, share * own_rows, wide), jnp.float32),
-            pltpu.VMEM((cols // wide, tensor, share * own_rows, wide), jnp.float32),
+            pltpu.VMEM((blocks, layers, seq, 2 * genomes * rows_dev, wide_cols // 2), jnp.bfloat16),
+            pltpu.VMEM((layers, cols // wide, tensor, share * genomes * rows_dev, wide), jnp.float32),
+            pltpu.VMEM((layers, cols // wide, tensor, share * genomes * rows_dev, wide), jnp.float32),
             pltpu.VMEM((layers, genomes, share * rows_dev, cols), jnp.float32),
             dma((blocks, layers, seq)), dma((blocks, layers, seq)),
-            dma((blocks, seq)), dma((blocks, seq)),
-            dma((cols // wide, tensor)), dma((cols // wide, tensor)),
+            dma((blocks, layers, seq)), dma((blocks, layers, seq)),
+            dma((layers, cols // wide, tensor)), dma((layers, cols // wide, tensor)),
         ],
         compiler_params=pltpu.CompilerParams(
             collective_id=0, has_side_effects=True, vmem_limit_bytes=60 * 1024 * 1024),

time: 57.1 us -> 55.3 us (0.968); the launches traced: 56 us -> 55.1 us
  Pallas kernels: 53.9 us -> 53 us
    pallas_call x1, Pallas kernels: 53.9 us -> 53 us  [shards(): pl.pallas_call(functools.partial(kernel, seq, tensor, granule, bits), out...]
where the time goes in v4:
time: 55.3 us; the launch traced here: 55.1 us
  Pallas kernels  53 us (96%)
  local copies, waits for them, and re-layouts  1.47 us (3%)
  between operations  0.66 us (1%)
    pallas_call x1, Pallas kernels, shards(): pl.pallas_call(functools.partial(kernel, seq, tensor, granule, bits), out...  53 us
    unnamed x1, local copies, waits for them, and re-layouts  1.47 us

profile of v4, /device:TPU:0, one launch (start us, length us, event | category | flops | bytes accessed | tf_op | source)
XLA Modules:
  0.0 55.1 jit_solution(2502299042753032768)
XLA Ops:
  0.7 53.0 %shard_map.82 = bf16[2,2,8,1024]{3,2,1,0:T(8,128)(2,1)} custom-call(s32[2]{0:T(128)} %lengths.1, s32[1]{0:T(128)S(6)} %copy.10.tile_index, f32[2,16,2048]{2,1,0:T(8,128)} %rates.1, f32[2,16,2048]{2,1,0:T(8,128)} %residues.1, f32[2,16,2048]{2,1,0:T(8,128)} %freqs.1, bf16[2,2,4,2048]{3,2,1,0:T(4,128)(2,1)} %gates.1, bf16[2,2,256,2048]{3,2,1,0:T(8,128)(2,1)} %hist_hbm.1, ...), custom_call_target="tpu_custom_call" | custom-call | tf_op jit(solution)/shard_map/pallas_call | solution.py:335
  53.7 1.5 %copy.11 = bf16[2,2,8,1024]{3,2,1,0:T(8,128)(2,1)} copy(bf16[2,2,8,1024]{3,2,1,0:T(8,128)(2,1)} %shard_map.82) | data formatting | bytes 131072

commit v5 on v4

--- a/solution.py
+++ b/solution.py
@@ -13,7 +13,7 @@
 SUB = 8
 LANE = 128
 GROUP = 4
-STEPS = 32
+STEPS = 64
 RUN = 32
 
 
@@ -47,7 +47,7 @@
     genomes, span = x_ref.shape[:2]
     modes = params[0].shape[1]
     rows = acc.shape[1]
-    chunk = 32
+    chunk = STEPS // 2
     wide_cols = SUB * LANE
     for i, ref in enumerate(params):
         spread_rows(pars.at[i], 0, ref[l, :, pl.ds(pl.multiple_of(c * wide_cols, wide_cols), wide_cols)])
@@ -55,13 +55,17 @@
     for g in range(genomes):
         ahead = jnp.full((SUB, LANE), starts[g] - first, jnp.int32)
         live = jnp.minimum(jnp.maximum(ahead, 0), span)
-        blocks_live.append(live)
+        blocks_live.append(live + (live & chunk))
+        count = jnp.minimum(jnp.maximum(starts[g] - first, 0), span)
+        odd = (jnp.full((chunk, wide_cols), count, jnp.int32) & chunk) != 0
         hops.append(jnp.maximum(ahead - live, 0))
 
         @pl.loop(0, span // chunk)
         def _(q):
             block = x_ref[g, pl.ds(pl.multiple_of(q * chunk, chunk), chunk), :]
-            spread_rows(xs.at[g], q * (chunk * SUB), block.astype(jnp.float32))
+            before = x_ref[g, pl.ds(pl.multiple_of(jnp.maximum(q - 1, 0) * chunk, chunk), chunk), :]
+            before = before.astype(jnp.float32) * jnp.minimum(q, 1).astype(jnp.float32)
+            spread_rows(xs.at[g], q * (chunk * SUB), jnp.where(odd, before, block.astype(jnp.float32)))
 
     acc[...] = jnp.zeros_like(acc)
     wide = GROUP * SUB

time: 55.3 us -> 54.6 us (0.987)
  Pallas kernels: 53 us -> 52.3 us
    pallas_call x1, Pallas kernels: 53 us -> 52.3 us  [shards(): pl.pallas_call(functools.partial(kernel, seq, tensor, granule, bits), out...]
where the time goes in v5:
time: 54.6 us; the launch traced here: 54.4 us
  Pallas kernels  52.3 us (96%)
  local copies, waits for them, and re-layouts  1.47 us (3%)
  between operations  0.66 us (1%)
    pallas_call x1, Pallas kernels, shards(): pl.pallas_call(functools.partial(kernel, seq, tensor, granule, bits), out...  52.3 us
    unnamed x1, local copies, waits for them, and re-layouts  1.47 us

profile of v5, /device:TPU:0, one launch (start us, length us, event | category | flops | bytes accessed | tf_op | source)
XLA Modules:
  0.0 54.4 jit_solution(16017030125283291836)
XLA Ops:
  0.7 52.3 %shard_map.82 = bf16[2,2,8,1024]{3,2,1,0:T(8,128)(2,1)} custom-call(s32[2]{0:T(128)} %lengths.1, s32[1]{0:T(128)S(6)} %copy.10.tile_index, f32[2,16,2048]{2,1,0:T(8,128)} %rates.1, f32[2,16,2048]{2,1,0:T(8,128)} %residues.1, f32[2,16,2048]{2,1,0:T(8,128)} %freqs.1, bf16[2,2,4,2048]{3,2,1,0:T(4,128)(2,1)} %gates.1, bf16[2,2,256,2048]{3,2,1,0:T(8,128)(2,1)} %hist_hbm.1, ...), custom_call_target="tpu_custom_call" | custom-call | tf_op jit(solution)/shard_map/pallas_call | solution.py:339
  52.9 1.5 %copy.11 = bf16[2,2,8,1024]{3,2,1,0:T(8,128)(2,1)} copy(bf16[2,2,8,1024]{3,2,1,0:T(8,128)(2,1)} %shard_map.82) | data formatting | bytes 131072
